TPU v7x, 32 devices: a whole 2x2x4 slice. The times are simulated.
32 devices in a mesh: cent: 4 (over y, core), pass: 8 (over z, x).
Axes of the slice: x: 2, y: 2, z: 4, core: 2. Of those that a mesh axis runs over, the one named last changes fastest.
Arguments:
- queries: float32 [32, 32, 128], P('cent'), may hold values from -0.6 to 0.6
- centroids: float32 [262144, 128], P(('cent', 'pass')), may hold values from -0.6 to 0.6
- bucket_weights: float32 [4, 128], replicated, may hold values from -0.6 to 0.6
- touched: int32 [8, 4096], replicated, may hold values from 0 to 262143, as said below
- token_codes: int32 [4096, 64], P('pass'), may hold values from 0 to 4095
- residual_bits: int32 [4096, 2048], P('pass'), may hold values from 0 to 255
- candidate_blocks: int32 [32, 8, 32], P('cent', 'pass'), may hold values from 0 to 31, as said below
- block_counts: int32 [32, 8], P('cent', 'pass'), may hold values from 12 to 32, as said below
Outputs:
- candidate_scores: float32 [32, 8, 512], P('cent', 'pass')
- top_scores: float32 [32, 32], P('cent')
Inputs may be any that keep to these rules, and one draw needn't show every extreme that they name: For every shard p and range r < 32, touched[p, r*128 + t] for t < 128 are distinct ids from r*8192 to (r+1)*8192 - 1. `candidate_blocks`: the 32 block ids of one query on one shard are distinct; entries past the count are valid ids that are not live. `block_counts`: every query has exactly 32 live blocks on some shard.
All inputs are finite; a program needn't handle non-finite values.
Results may differ from a plain program's by a relative error of at most 0.0003.
Values sent between devices are 32-bit elements; how exact they have to be, the bound alone decides.
A program may use at most 192 MiB of HBM per device.

v0:
```python
import jax
import jax.numpy as jnp
from jax import lax
from jax.sharding import PartitionSpec as P

BLK = 16
KTOP = 32


floor_value = -1e30


def score_queries(queries, table, shard_codes, shard_bits, bucket_weights, blocks, live_counts):
    query_count, query_len, width = queries.shape
    block_count = blocks.shape[1]
    passage_len = shard_codes.shape[1]
    word_count = shard_bits.shape[1] // passage_len
    slot_count = block_count * BLK
    shifts = 2 * jnp.arange(4, dtype=jnp.int32)

    def one_query(index):
        block_ids = lax.dynamic_index_in_dim(blocks, index, 0, keepdims=False)
        passage_rows = (
            block_ids[:, None] * BLK + jnp.arange(BLK, dtype=jnp.int32)[None, :]
        ).reshape(-1)
        local_codes = jnp.take(shard_codes, passage_rows, axis=0).reshape(-1)
        packed = jnp.take(shard_bits, passage_rows, axis=0).reshape(-1, word_count)
        levels = jnp.bitwise_and(
            jnp.right_shift(packed[:, :, None], shifts[None, None, :]), 3
        ).reshape(-1, width)
        residual = jnp.where(
            levels == 0,
            bucket_weights[0],
            jnp.where(
                levels == 1,
                bucket_weights[1],
                jnp.where(levels == 2, bucket_weights[2], bucket_weights[3]),
            ),
        )
        query_rows = lax.dynamic_index_in_dim(queries, index, 0, keepdims=False)
        table_rows = lax.dynamic_slice_in_dim(table, index * query_len, query_len, 0)
        looked = jnp.take(table_rows, local_codes, axis=1)
        token_scores = looked + jnp.dot(query_rows, residual.T, precision=lax.Precision.HIGHEST)
        best = jnp.sum(
            jnp.max(token_scores.reshape(query_len, slot_count, passage_len), axis=2), axis=0
        )
        live = lax.dynamic_index_in_dim(live_counts, index, 0, keepdims=False)
        valid = jnp.arange(slot_count, dtype=jnp.int32) // BLK < live
        return (
            jnp.where(valid, best, jnp.zeros((), jnp.float32)),
            jnp.where(valid, best, jnp.full((), floor_value, jnp.float32)),
        )

    return lax.map(one_query, jnp.arange(query_count, dtype=jnp.int32))


def body(
    queries,
    centroids,
    bucket_weights,
    touched,
    token_codes,
    residual_bits,
    candidate_blocks,
    block_counts,
):
    group_queries, query_len, width = queries.shape
    pass_count = lax.axis_size("pass")
    cent_count = lax.axis_size("cent")
    row_count = centroids.shape[0]
    per_range = touched.shape[1] // (pass_count * cent_count)
    owner = lax.axis_index("cent") * pass_count + lax.axis_index("pass")
    wanted = lax.dynamic_slice_in_dim(touched, owner * per_range, per_range, 1) - owner * row_count
    picked = jnp.take(centroids, wanted.reshape(-1), axis=0)
    all_queries = lax.all_gather(queries, "cent", axis=0, tiled=True)
    grouped = all_queries.reshape(cent_count, group_queries * query_len, width)
    picked_rows = picked.reshape(pass_count, per_range, width)
    outgoing = jnp.einsum("cqd,pud->qcpu", grouped, picked_rows, precision=lax.Precision.HIGHEST)
    arrived = lax.all_to_all(
        lax.all_to_all(outgoing, "cent", split_axis=1, concat_axis=1, tiled=True),
        "pass",
        split_axis=2,
        concat_axis=2,
        tiled=True,
    )
    table = arrived.reshape(group_queries * query_len, -1)
    plain, masked = score_queries(
        queries,
        table,
        token_codes,
        residual_bits,
        bucket_weights,
        candidate_blocks[:, 0, :],
        block_counts[:, 0],
    )
    candidate_scores = plain[:, None, :]
    every_score = lax.all_gather(masked, "pass", axis=1, tiled=True)
    top_scores = lax.top_k(every_score, KTOP)[0]
    return (candidate_scores, top_scores)


def solution(mesh):
    placed = (
        P("cent", None, None),
        P(("cent", "pass"), None),
        P(),
        P(),
        P("pass", None),
        P("pass", None),
        P("cent", "pass", None),
        P("cent", "pass"),
    )
    return jax.shard_map(
        body,
        mesh=mesh,
        in_specs=placed,
        out_specs=(P("cent", "pass", None), P("cent", None)),
        check_vma=False,
    )
```

profile of v0, /device:TPU:0, one launch (start us, length us, event | category | flops | bytes accessed | tf_op | source)
XLA Modules:
  0.0 2154.1 jit_solution(11331438554176172419)
XLA Ops:
  19.3 50.7 %all_to_all.10 = f32[256,4,8,128]{0,3,2,1:T(8,128)S(1)} all-to-all(f32[256,4,8,128]{0,3,2,1:T(8,128)S(1)} %copy.28), channel_id=1, replica_groups=mesh['cent'=4,'pass'=8] {'cent'}, dimensions={1} | all-to-all | bytes 8388608 | tf_op jit(solution)/shard_map/all_to_all | solution.py:80
  78.5 92.8 %all-to-all-done.1 = f32[256,4,8,128]{0,3,1,2:T(8,128)} async-done(((f32[256,4,8,128]{0,3,1,2:T(8,128)}), f32[256,4,8,128]{0,3,1,2:T(8,128)}, u32[]{:S(2)}, u32[]{:S(2)}) %all-to-all-start.1) | async-done | bytes 4194336 | tf_op jit(solution)/shard_map/all_to_all | solution.py:79
  175.9 1935.8 %while.15 = (s32[]{:T(128)}, f32[8,512]{1,0:T(8,128)S(1)}, f32[8,512]{1,0:T(8,128)S(1)}, s32[8]{0:T(128)S(1)}, s32[8]{0:T(128)S(1)}, /*index=5*/s32[8,32]{1,0:T(...) while((s32[]{:T(128)}, f32[8,512]{1,0:T(8,128)S(1)}, ...), condition=%wide.region_3.4_spmd.clone, body=%wide.region_0.3_spmd.clone.sunk | while | flops 1648765952 | bytes 145922240 | solution.py:54
  251.6 19.4 select_n.320
  271.0 108.2 %gather_fusion.2 = f32[32768,32]{1,0:T(8,128)} fusion(f32[32,4096]{0,1:T(8,128)S(1)} %constant_dynamic-slice_fusion.3, s32[32768]{0:T(1024)S(1)} %broadcast_clamp_fusion.3), kind=kCustom, calls=%fused_computation.1.clone.clone.1 | custom fusion | bytes 8519680 | tf_op jit(solution)/shard_map/while/body/eval_jaxpr/jit(_take)/gather | solution.py:42
  493.6 19.4 select_n.320
  513.0 108.2 %gather_fusion.2 = f32[32768,32]{1,0:T(8,128)} fusion(f32[32,4096]{0,1:T(8,128)S(1)} %constant_dynamic-slice_fusion.3, s32[32768]{0:T(1024)S(1)} %broadcast_clamp_fusion.3), kind=kCustom, calls=%fused_computation.1.clone.clone.1 | custom fusion | bytes 8519680 | tf_op jit(solution)/shard_map/while/body/eval_jaxpr/jit(_take)/gather | solution.py:42
  688.4 19.1 broadcast_select_fusion.5
  735.6 19.4 select_n.320
  755.0 108.2 %gather_fusion.2 = f32[32768,32]{1,0:T(8,128)} fusion(f32[32,4096]{0,1:T(8,128)S(1)} %constant_dynamic-slice_fusion.3, s32[32768]{0:T(1024)S(1)} %broadcast_clamp_fusion.3), kind=kCustom, calls=%fused_computation.1.clone.clone.1 | custom fusion | bytes 8519680 | tf_op jit(solution)/shard_map/while/body/eval_jaxpr/jit(_take)/gather | solution.py:42
  930.3 19.1 broadcast_select_fusion.5
  977.5 19.4 select_n.320
  996.9 108.2 %gather_fusion.2 = f32[32768,32]{1,0:T(8,128)} fusion(f32[32,4096]{0,1:T(8,128)S(1)} %constant_dynamic-slice_fusion.3, s32[32768]{0:T(1024)S(1)} %broadcast_clamp_fusion.3), kind=kCustom, calls=%fused_computation.1.clone.clone.1 | custom fusion | bytes 8519680 | tf_op jit(solution)/shard_map/while/body/eval_jaxpr/jit(_take)/gather | solution.py:42
  1219.5 19.4 select_n.320
  1238.9 108.2 %gather_fusion.2 = f32[32768,32]{1,0:T(8,128)} fusion(f32[32,4096]{0,1:T(8,128)S(1)} %constant_dynamic-slice_fusion.3, s32[32768]{0:T(1024)S(1)} %broadcast_clamp_fusion.3), kind=kCustom, calls=%fused_computation.1.clone.clone.1 | custom fusion | bytes 8519680 | tf_op jit(solution)/shard_map/while/body/eval_jaxpr/jit(_take)/gather | solution.py:42
  1461.4 19.4 select_n.320
  1480.8 108.2 %gather_fusion.2 = f32[32768,32]{1,0:T(8,128)} fusion(f32[32,4096]{0,1:T(8,128)S(1)} %constant_dynamic-slice_fusion.3, s32[32768]{0:T(1024)S(1)} %broadcast_clamp_fusion.3), kind=kCustom, calls=%fused_computation.1.clone.clone.1 | custom fusion | bytes 8519680 | tf_op jit(solution)/shard_map/while/body/eval_jaxpr/jit(_take)/gather | solution.py:42
  1656.2 19.1 broadcast_select_fusion.5
  1703.4 19.4 select_n.320
  1722.8 108.2 %gather_fusion.2 = f32[32768,32]{1,0:T(8,128)} fusion(f32[32,4096]{0,1:T(8,128)S(1)} %constant_dynamic-slice_fusion.3, s32[32768]{0:T(1024)S(1)} %broadcast_clamp_fusion.3), kind=kCustom, calls=%fused_computation.1.clone.clone.1 | custom fusion | bytes 8519680 | tf_op jit(solution)/shard_map/while/body/eval_jaxpr/jit(_take)/gather | solution.py:42
  1898.2 19.1 broadcast_select_fusion.5
  1945.3 19.4 select_n.320
  1964.7 108.2 %gather_fusion.2 = f32[32768,32]{1,0:T(8,128)} fusion(f32[32,4096]{0,1:T(8,128)S(1)} %constant_dynamic-slice_fusion.3, s32[32768]{0:T(1024)S(1)} %broadcast_clamp_fusion.3), kind=kCustom, calls=%fused_computation.1.clone.clone.1 | custom fusion | bytes 8519680 | tf_op jit(solution)/shard_map/while/body/eval_jaxpr/jit(_take)/gather | solution.py:42
  2112.4 30.5 %all_gather.7 = f32[8,4096]{1,0:T(8,128)S(1)} all-gather(f32[8,512]{1,0:T(8,128)S(1)} %get-tuple-element.157), channel_id=1, replica_groups=mesh['cent'=4,'pass'=8] {'pass'}, dimensions={1}, use_global_device_ids=true | all-gather | bytes 147456 | tf_op jit(solution)/shard_map/all_gather | solution.py:97
  (323 shorter events, 860.1 us)
Async XLA Ops:
  72.3 5.9 copy-start
  72.3 98.9 %all-to-all-start.1 = ((f32[256,4,8,128]{0,3,1,2:T(8,128)}), f32[256,4,8,128]{0,3,1,2:T(8,128)}, u32[]{:S(2)}, u32[]{:S(2)}) async-start(f32[256,4,8,128]{0,3,1,2:T(8,128)} %copy.29), calls=%async_computation.1 | async-start | bytes 8388608 | tf_op jit(solution)/shard_map/all_to_all | solution.py:79
  78.4 97.5 %copy-start.1 = (f32[4,128]{1,0:T(4,128)S(1)}, f32[4,128]{1,0:T(4,128)}, u32[]{:S(2)}) copy-start(f32[4,128]{1,0:T(4,128)} %param.12) | copy-start | bytes 6148
  78.4 97.5 %copy-start.2 = (s32[8,1]{0,1:T(1,128)S(1)}, s32[8,1]{0,1:T(1,128)}, u32[]{:S(2)}) copy-start(s32[8,1]{0,1:T(1,128)} %param.17) | copy-start | bytes 100
where the time goes:
time: 2170 us; the launch traced here: 2150 us
  local copies, waits for them, and re-layouts  1480 us (68%)
  other arithmetic  356 us (16%)
  matrix products  111 us (5%)
  waiting for transfers between devices  92.8 us (4%)
  blocking collectives  90.1 us (4%)
  loops' own time  22.4 us (1%)
    gather x16, local copies, waits for them, and re-layouts, one_query(): looked = jnp.take(table_rows, local_codes, axis=1)  958 us
    select_n x8, local copies, waits for them, and re-layouts, one_query(): jnp.where(levels == 0, bucket_weights[0], jnp.where(levels == 1, bucket_w...  155 us
    select_n x8, other arithmetic, one_query(): packed = jnp.take(shard_bits, passage_rows, axis=0).reshape(-1, word_count)  153 us
    gather x16, local copies, waits for them, and re-layouts, one_query(): packed = jnp.take(shard_bits, passage_rows, axis=0).reshape(-1, word_count)  152 us
    select_n x8, other arithmetic, one_query(): jnp.where(levels == 0, bucket_weights[0], jnp.where(levels == 1, bucket_w...  132 us
    dot_general x8, matrix products, one_query(): jnp.dot(query_rows, residual.T, precision=lax.Precision.HIGHEST)  107 us
    select_n x8, local copies, waits for them, and re-layouts, one_query(): packed = jnp.take(shard_bits, passage_rows, axis=0).reshape(-1, word_count)  92.8 us
    all_to_all x1, waiting for transfers between devices, body(): lax.all_to_all(lax.all_to_all(outgoing, 'cent', split_axis=1, concat_axis...  92.8 us
  transfers between devices with their start and end apart: 1, of which 1 were waited for; matrix products, arithmetic and copies ran while one was open for 0% of the time, Pallas kernels for 0%

commit v1 on v0

v1 whole, which is shorter than its diff:
```python
import functools

import jax
import jax.numpy as jnp
from jax import lax
from jax.experimental import pallas as pl
from jax.experimental.pallas import tpu as pltpu
from jax.sharding import PartitionSpec as P

BLK = 16
KTOP = 32
CHUNK = 16

floor_value = -1e30


def pick_kernel(count, wanted_ref, rows_ref, out_ref):
    def some(step, carry):
        base = pl.multiple_of(step * 16, 16)
        for k in range(16):
            row = wanted_ref[base + k]
            out_ref[pl.ds(base + k, 1), :] = rows_ref[pl.ds(row, 1), :]
        return carry

    lax.fori_loop(0, count // 16, some, 0)


def pick_rows(centroids, wanted):
    count = wanted.shape[0]
    width = centroids.shape[1]
    return pl.pallas_call(
        functools.partial(pick_kernel, count),
        out_shape=jax.ShapeDtypeStruct((count, width), jnp.float32),
        in_specs=[
            pl.BlockSpec(memory_space=pltpu.SMEM),
            pl.BlockSpec(memory_space=pltpu.VMEM),
        ],
        out_specs=pl.BlockSpec(memory_space=pltpu.VMEM),
        compiler_params=pltpu.CompilerParams(vmem_limit_bytes=24 * 2**20),
    )(wanted, centroids)


def score_kernel(
    passage_len, where_ref, codes_ref, bits_ref, weights_ref, query_ref, fold_ref, table_ref, out_ref, held
):
    chunk = pl.program_id(0)
    width = weights_ref.shape[1]
    rows = passage_len * CHUNK
    words = width // 4
    per_tile = width // words

    def some(step, carry):
        base = pl.multiple_of(step * CHUNK, CHUNK)
        for k in range(CHUNK):
            code = codes_ref[chunk * rows + base + k]
            held[pl.ds(base + k, 1), :] = table_ref[pl.ds(code, 1), :]
        return carry

    lax.fori_loop(0, passage_len, some, 0, unroll=4)

    tiles = passage_len // per_tile
    packed = jnp.concatenate(
        [bits_ref[:, i * width : (i + 1) * width] for i in range(tiles)], axis=0
    )
    source = lax.broadcasted_iota(jnp.int32, (width, width * per_tile), 0)
    target = lax.broadcasted_iota(jnp.int32, (width, width * per_tile), 1)
    spread = jnp.where(target // 4 == source, 1.0, 0.0).astype(jnp.bfloat16)
    wide = jnp.dot(
        packed.astype(jnp.float32).astype(jnp.bfloat16), spread, preferred_element_type=jnp.float32
    ).astype(jnp.int32)
    shift = 2 * (lax.broadcasted_iota(jnp.int32, (1, width), 1) % 4)
    parts = []
    for a in range(per_tile):
        level = jnp.right_shift(wide[:, a * width : (a + 1) * width], shift) & 3
        value = jnp.where(
            level == 0,
            weights_ref[0:1, :],
            jnp.where(
                level == 1,
                weights_ref[1:2, :],
                jnp.where(level == 2, weights_ref[2:3, :], weights_ref[3:4, :]),
            ),
        )
        parts.append(value.reshape(tiles, 1, CHUNK, width))
    residual = jnp.concatenate(parts, axis=1).reshape(rows, width)
    token = (held[...] + residual).astype(jnp.bfloat16)
    token = jnp.concatenate([token, token], axis=1)
    score = jnp.dot(token, query_ref[...], preferred_element_type=jnp.float32)
    best = jnp.max(score.reshape(passage_len, CHUNK, score.shape[1]), axis=0)
    out_ref[...] = lax.dot_general(
        best,
        fold_ref[...],
        (((1,), (0,)), ((), ())),
        precision=lax.Precision.HIGHEST,
        preferred_element_type=jnp.float32,
    )


def score_passages(all_queries, table, codes, bits, weights, where, mine):
    query_count, query_len, width = all_queries.shape
    passage_len = codes.shape[0] // mine
    flat = all_queries.reshape(query_count * query_len, width)
    high = lax.reduce_precision(flat, 8, 7)
    both = jnp.concatenate([high, flat - high], axis=1).T.astype(jnp.bfloat16)
    fold = (
        jnp.arange(query_count * query_len)[:, None] // query_len == jnp.arange(query_count)[None, :]
    ).astype(jnp.float32)
    chunks = mine // CHUNK
    whole = pl.Buffered(buffer_count=1)
    return pl.pallas_call(
        functools.partial(score_kernel, passage_len),
        out_shape=jax.ShapeDtypeStruct((mine, query_count), jnp.float32),
        grid_spec=pltpu.PrefetchScalarGridSpec(
            num_scalar_prefetch=2,
            grid=(chunks,),
            in_specs=[
                pl.BlockSpec((CHUNK, bits.shape[1]), lambda c, w, k: (w[0] * chunks + c, 0)),
                pl.BlockSpec(weights.shape, lambda c, w, k: (0, 0)),
                pl.BlockSpec(both.shape, lambda c, w, k: (0, 0), pipeline_mode=whole),
                pl.BlockSpec(fold.shape, lambda c, w, k: (0, 0), pipeline_mode=whole),
                pl.BlockSpec(table.shape, lambda c, w, k: (0, 0), pipeline_mode=whole),
            ],
            out_specs=pl.BlockSpec((CHUNK, query_count), lambda c, w, k: (c, 0)),
            scratch_shapes=[pltpu.VMEM((passage_len * CHUNK, width), jnp.float32)],
        ),
        compiler_params=pltpu.CompilerParams(vmem_limit_bytes=48 * 2**20),
    )(where, codes, bits, weights, both, fold, table)


def largest(values, keep):
    count = values.shape[1]
    place = jnp.arange(count, dtype=jnp.int32)
    one, other = values[:, :, None], values[:, None, :]
    ahead = (other > one) | ((other == one) & (place[None, None, :] < place[None, :, None]))
    rank = jnp.sum(ahead.astype(jnp.int32), axis=2)
    hit = rank[:, None, :] == jnp.arange(keep, dtype=jnp.int32)[None, :, None]
    return jnp.sum(jnp.where(hit, values[:, None, :], 0.0), axis=2)


def body(
    queries,
    centroids,
    bucket_weights,
    touched,
    token_codes,
    residual_bits,
    candidate_blocks,
    block_counts,
):
    group_queries, query_len, width = queries.shape
    pass_count = lax.axis_size("pass")
    cent_count = lax.axis_size("cent")
    row_count = centroids.shape[0]
    cent = lax.axis_index("cent").astype(jnp.int32)
    per_range = touched.shape[1] // (pass_count * cent_count)
    owner = cent * pass_count + lax.axis_index("pass")
    wanted = lax.dynamic_slice_in_dim(touched, owner * per_range, per_range, 1) - owner * row_count
    picked = pick_rows(centroids, wanted.reshape(-1))
    all_queries = lax.all_gather(queries, "cent", axis=0, tiled=True)
    arrived = lax.all_to_all(
        picked.reshape(pass_count, per_range, width), "pass", split_axis=0, concat_axis=0, tiled=True
    )
    table = lax.all_gather(arrived, "cent", axis=0, tiled=True).reshape(-1, width)

    passages, passage_len = token_codes.shape
    mine = passages // cent_count
    codes = lax.dynamic_slice_in_dim(token_codes, cent * mine, mine, 0)
    codes = codes.reshape(mine // CHUNK, CHUNK, passage_len).transpose(0, 2, 1).reshape(-1)
    scored = score_passages(
        all_queries, table, codes, residual_bits, bucket_weights, cent.reshape(1), mine
    )
    every = lax.all_to_all(scored.T, "cent", split_axis=0, concat_axis=1, tiled=True)

    blocks = candidate_blocks[:, 0, :]
    block_count = blocks.shape[1]
    stored = passages // BLK
    by_block = every.reshape(group_queries, 1, stored, BLK)
    chosen = blocks[:, :, None, None] == jnp.arange(stored, dtype=jnp.int32)[None, None, :, None]
    slots = jnp.sum(jnp.where(chosen, by_block, 0.0), axis=2)
    live = jnp.arange(block_count, dtype=jnp.int32)[None, :, None] < block_counts[:, :, None]
    plain = jnp.where(live, slots, 0.0).reshape(group_queries, -1)
    masked = jnp.where(live, slots, floor_value).reshape(group_queries, -1)
    local_top = largest(masked, KTOP)
    every_top = lax.all_gather(local_top, "pass", axis=1, tiled=True)
    return plain[:, None, :], largest(every_top, KTOP)


def solution(mesh):
    placed = (
        P("cent", None, None),
        P(("cent", "pass"), None),
        P(),
        P(),
        P("pass", None),
        P("pass", None),
        P("cent", "pass", None),
        P("cent", "pass"),
    )
    return jax.shard_map(
        body,
        mesh=mesh,
        in_specs=placed,
        out_specs=(P("cent", "pass", None), P("cent", None)),
        check_vma=False,
    )
```

time: 2170 us -> 127 us (0.06)
  local copies, waits for them, and re-layouts: 1480 us -> 6.15 us
  other arithmetic: 356 us -> 6.08 us
  matrix products: 111 us -> 0 us
  waiting for transfers between devices: 92.8 us -> 17.1 us
  blocking collectives: 90.1 us -> 59.5 us
  loops' own time: 22.4 us -> 0 us
    gather x49 -> x0, local copies, waits for them, and re-layouts: 1120 us -> none  [the longest x16 958 us: one_query(): looked = jnp.take(table_rows, local_codes, axis=1)]
    select_n x50 -> x2, other arithmetic: 292 us -> 0.11 us  [the longest x1 0.1 us: body(): masked = jnp.where(live, slots, floor_value).reshape(group_queries, -1)]
    select_n x24 -> x2, local copies, waits for them, and re-layouts: 249 us -> 0.83 us  [the longest x1 0.72 us: body(): plain = jnp.where(live, slots, 0.0).reshape(group_queries, -1)]
    dot_general x9 -> x0, matrix products: 111 us -> none  [the longest x8 107 us: one_query(): jnp.dot(query_rows, residual.T, precision=lax.Precision.HIGHEST)]
    all_to_all x1, waiting for transfers between devices: 92.8 us -> 3.79 us  [body(): lax.all_to_all(scored.T, 'cent', split_axis=0, concat_axis=1, tiled=True)]
    reshape x8 -> x2, local copies, waits for them, and re-layouts: 58.8 us -> 0.33 us  [the longest x1 0.19 us: score_passages(): flat = all_queries.reshape(query_count * query_len, width)]
    reduce_max x8 -> x0, other arithmetic: 44.9 us -> none  [one_query(): jnp.max(token_scores.reshape(query_len, slot_count, passage_len), axis=2)]
    all_to_all x1, blocking collectives: 50.7 us -> 21.8 us  [body(): lax.all_to_all(picked.reshape(pass_count, per_range, width), 'pass', spli...]
  transfers between devices with their start and end apart: 1 -> 2, of which waited for: 1 -> 2; matrix products, arithmetic and copies ran while one was open for 0% -> 1% of each run, Pallas kernels for 0% -> 0%
where the time goes in v1:
time: 127 us; the launch traced here: 126 us
  blocking collectives  59.5 us (47%)
  Pallas kernels  19.8 us (16%)
  waiting for transfers between devices  17.1 us (13%)
  between operations  14.3 us (11%)
  local copies, waits for them, and re-layouts  6.15 us (5%)
  other arithmetic  6.08 us (5%)
  starting transfers between devices  3.29 us (3%)
    all_gather x1, blocking collectives, body(): every_top = lax.all_gather(local_top, 'pass', axis=1, tiled=True)  30.5 us
    all_to_all x1, blocking collectives, body(): lax.all_to_all(picked.reshape(pass_count, per_range, width), 'pass', spli...  21.8 us
    pallas_call x1, Pallas kernels, score_passages(): pl.pallas_call(functools.partial(score_kernel, passage_len), out_shape=ja...  18.1 us
    all_gather x1, waiting for transfers between devices, body(): lax.all_gather(arrived, 'cent', axis=0, tiled=True).reshape(-1, width)  13.3 us
    all_gather x1, blocking collectives, body(): all_queries = lax.all_gather(queries, 'cent', axis=0, tiled=True)  7.22 us
    unnamed x16, local copies, waits for them, and re-layouts  3.98 us
    all_to_all x1, waiting for transfers between devices, body(): lax.all_to_all(scored.T, 'cent', split_axis=0, concat_axis=1, tiled=True)  3.79 us
    all_to_all x1, starting transfers between devices, body(): lax.all_to_all(scored.T, 'cent', split_axis=0, concat_axis=1, tiled=True)  3.25 us
  transfers between devices with their start and end apart: 2, of which 2 were waited for; matrix products, arithmetic and copies ran while one was open for 1% of the time, Pallas kernels for 0%

profile of v1, /device:TPU:0, one launch (start us, length us, event | category | flops | bytes accessed | tf_op | source)
XLA Modules:
  0.0 126.2 jit_solution(18180670182988195850)
XLA Ops:
  7.2 0.7 subtract_bitcast_fusion.wanted_ref
  7.9 2.2 %copy-done.1 = f32[8192,128]{1,0:T(8,128)S(1)} copy-done((f32[8192,128]{1,0:T(8,128)S(1)}, f32[8192,128]{1,0:T(8,128)}, u32[]{:S(2)}) %copy-start.1) | copy-done | bytes 4194328
  10.1 1.7 %shard_map.98 = f32[1024,128]{1,0:T(8,128)S(1)} custom-call(s32[1024]{0:T(1024)S(1)} %subtract_bitcast_fusion.wanted_ref, f32[8192,128]{1,0:T(8,128)S(1)} %copy-done.1), custom_call_target="tpu_custom_call" | custom-call | tf_op jit(solution)/shard_map/pallas_call | solution.py:31
  11.8 21.8 %all_to_all.21 = f32[8,128,128]{2,1,0:T(8,128)} all-to-all(f32[8,128,128]{2,1,0:T(8,128)S(1)} %bitcast.23), channel_id=1, replica_groups=mesh['cent'=4,'pass'=8] {'pass'}, dimensions={0} | all-to-all | bytes 1048576 | tf_op jit(solution)/shard_map/all_to_all | solution.py:160
  33.8 0.1 copy.30
  33.9 0.1 reshape.184.codes_ref
  34.1 7.2 %all_gather.9 = f32[32,32,128]{2,1,0:T(8,128)S(1)} all-gather(f32[8,32,128]{2,1,0:T(8,128)S(1)} %copy-done.4), channel_id=1, replica_groups=mesh['cent'=4,'pass'=8] {'cent'}, dimensions={0}, use_global_device_ids=true | all-gather | bytes 655360 | tf_op jit(solution)/shard_map/all_gather | solution.py:159
  41.3 0.2 copy.31
  41.9 0.2 fusion.1.fold_ref
  42.1 13.3 %all-gather.3.cloned.1.call-done = f32[32,128,128]{2,1,0:T(8,128)} async-done(((f32[8,128,128]{2,1,0:T(8,128)}), f32[32,128,128]{2,1,0:T(8,128)}) %all-gather.3.cloned.1.call-update) | async-done | bytes 2097168 | tf_op jit(solution)/shard_map/all_gather | solution.py:163
  55.4 1.6 %copy-done.2 = f32[32,128,128]{2,1,0:T(8,128)S(1)} copy-done((f32[32,128,128]{2,1,0:T(8,128)S(1)}, f32[32,128,128]{2,1,0:T(8,128)}, u32[]{:S(2)}) %copy-start.2) | copy-done | bytes 2097176
  57.0 18.1 %shard_map.99 = f32[128,32]{1,0:T(8,128)S(1)} custom-call(s32[1]{0:T(128)} %bitcast.2.where_ref, s32[8192]{0:T(1024)S(1)} %reshape.184.codes_ref, s32[512,2048]{1,0:T(8,128)} %bits_ref.1, f32[4,128]{1,0:T(4,128)S(1)} %copy-done.3, bf16[256,1024]{1,0:T(8,128)(2,1)S(1)} %maximum_bitcast_fusion.query_ref, f32[1024,32]{1,0:T(8,128)S(1)} %fusion.1.fold_ref, ...), custom_call_target="tpu_custom_call" | custom-call | tf_op jit(solution)/shard_map/pallas_call | solution.py:110
  75.1 0.7 copy.33
  75.8 3.3 %all-to-all-start.1 = ((f32[4,8,128]{2,1,0:T(8,128)}), f32[4,8,128]{2,1,0:T(8,128)S(1)}, u32[]{:S(2)}, u32[]{:S(2)}) async-start(f32[4,8,128]{2,1,0:T(8,128)} %bitcast.11), calls=%async_computation.1 | async-start | bytes 32768 | tf_op jit(solution)/shard_map/all_to_all | solution.py:172
  79.1 3.8 %all-to-all-done.1 = f32[4,8,128]{2,1,0:T(8,128)S(1)} async-done(((f32[4,8,128]{2,1,0:T(8,128)}), f32[4,8,128]{2,1,0:T(8,128)S(1)}, u32[]{:S(2)}, u32[]{:S(2)}) %all-to-all-start.1) | async-done | bytes 16416 | tf_op jit(solution)/shard_map/all_to_all | solution.py:172
  83.1 0.6 select_reduce_fusion
  83.7 0.1 broadcast_select_fusion
  83.9 0.1 select_n.63
  84.0 2.4 %convert_reduce_fusion = s32[8,512]{1,0:T(8,128)S(1)} fusion(f32[8,512]{1,0:T(8,128)S(1)} %select_n.63, pred[512,512]{1,0:T(8,128)(4,1)S(1)} %iota_compare_fusion), kind=kLoop, calls=%fused_computation | loop fusion | flops 12578816 | bytes 294912 | tf_op jit(solution)/shard_map/reduce_sum | solution.py:135
  86.4 0.1 select_reduce_fusion.1
  86.6 30.5 %all-gather = f32[8,32,8]{1,2,0:T(8,128)S(1)} all-gather(f32[1,32,8]{1,2,0:T(8,128)S(1)} %bitcast.30), channel_id=1, replica_groups=mesh['cent'=4,'pass'=8] {'pass'}, dimensions={0}, use_global_device_ids=true | all-gather | bytes 9216 | tf_op jit(solution)/shard_map/all_gather | solution.py:184
  117.1 0.8 convert_reduce_fusion.1
  117.9 0.7 select_reduce_fusion.2
  118.6 0.7 select_n.66
  (28 shorter events, 0.9 us)
Async XLA Ops:
  7.2 26.5 %copy-start = (s32[512,64]{0,1:T(8,128)S(1)}, s32[512,64]{0,1:T(8,128)}, u32[]{:S(2)}) copy-start(s32[512,64]{0,1:T(8,128)} %param.12) | copy-start | bytes 393220
  7.2 48.3 %all-gather.3.cloned.1.call-start = ((), (), s32[]{:S(2)}) async-start(), calls=%async_computation.2 | async-start | bytes 2621440 | tf_op jit(solution)/shard_map/all_gather | solution.py:163
  7.9 2.2 %copy-start.1 = (f32[8192,128]{1,0:T(8,128)S(1)}, f32[8192,128]{1,0:T(8,128)}, u32[]{:S(2)}) copy-start(f32[8192,128]{1,0:T(8,128)} %rows_ref.1) | copy-start | bytes 12582916
  11.8 22.3 %copy-start.4 = (f32[8,32,128]{2,1,0:T(8,128)S(1)}, f32[8,32,128]{2,1,0:T(8,128)}, u32[]{:S(2)}) copy-start(f32[8,32,128]{2,1,0:T(8,128)} %param.8) | copy-start | bytes 393220
  34.1 7.7 %copy-start.6 = (s32[8,1]{0,1:T(1,128)S(1)}, s32[8,1]{0,1:T(1,128)}, u32[]{:S(2)}) copy-start(s32[8,1]{0,1:T(1,128)} %param.15) | copy-start | bytes 100
  34.1 7.8 %copy-start.5 = (s32[8,1,32]{2,1,0:T(1,128)S(1)}, s32[8,1,32]{2,1,0:T(1,128)}, u32[]{:S(2)}) copy-start(s32[8,1,32]{2,1,0:T(1,128)} %param.14) | copy-start | bytes 3076
  41.3 14.1 %copy-start.3 = (f32[4,128]{1,0:T(4,128)S(1)}, f32[4,128]{1,0:T(4,128)}, u32[]{:S(2)}) copy-start(f32[4,128]{1,0:T(4,128)} %weights_ref.1) | copy-start | bytes 6148
  55.4 1.6 %copy-start.2 = (f32[32,128,128]{2,1,0:T(8,128)S(1)}, f32[32,128,128]{2,1,0:T(8,128)}, u32[]{:S(2)}) copy-start(f32[32,128,128]{2,1,0:T(8,128)} %all-gather.3.cloned.1.call-done) | copy-start | bytes 6291460
  75.8 7.1 %all-to-all-start.1 = ((f32[4,8,128]{2,1,0:T(8,128)}), f32[4,8,128]{2,1,0:T(8,128)S(1)}, u32[]{:S(2)}, u32[]{:S(2)}) async-start(f32[4,8,128]{2,1,0:T(8,128)} %bitcast.11), calls=%async_computation.1 | async-start | bytes 32768 | tf_op jit(solution)/shard_map/all_to_all | solution.py:172
Sparse Core Ops, SparseCore 0:
  33.8 21.6 all-gather.2

commit v2 on v1

--- a/solution.py
+++ b/solution.py
@@ -14,30 +14,237 @@
 floor_value = -1e30
 
 
-def pick_kernel(count, wanted_ref, rows_ref, out_ref):
-    def some(step, carry):
-        base = pl.multiple_of(step * 16, 16)
-        for k in range(16):
-            row = wanted_ref[base + k]
-            out_ref[pl.ds(base + k, 1), :] = rows_ref[pl.ds(row, 1), :]
+MESH = pl.DeviceIdType.MESH
+
+
+def meet(peers):
+    barrier = pltpu.get_barrier_semaphore()
+    for peer in peers:
+        pl.semaphore_signal(barrier, inc=1, device_id=peer, device_id_type=MESH)
+    pl.semaphore_wait(barrier, len(peers))
+
+
+def spread_kernel(
+    pass_count,
+    cent_count,
+    per_range,
+    wanted_ref,
+    rows_ref,
+    queries_ref,
+    table_ref,
+    all_ref,
+    picked,
+    out_sem,
+    in_sem,
+    query_out_sem,
+    query_in_sem,
+):
+    cent, own = lax.axis_index("cent"), lax.axis_index("pass")
+    core, pair = cent % 2, cent // 2
+    pairs = cent_count // 2
+    twin = (cent + 1 - 2 * core, own)
+    sides = [((pair + s) % pairs * 2 + core, own) for s in range(1, pairs)]
+    meet([(cent, (own + s) % pass_count) for s in range(1, pass_count)] + sides + [twin])
+
+    def send_query(slot, peer, source=None):
+        pltpu.make_async_remote_copy(
+            src_ref=all_ref.at[slot] if source is None else source,
+            dst_ref=all_ref.at[slot],
+            send_sem=query_out_sem,
+            recv_sem=query_in_sem.at[slot],
+            device_id=peer,
+            device_id_type=MESH,
+        ).start()
+
+    def send(source, slot, peer):
+        pltpu.make_async_remote_copy(
+            src_ref=source,
+            dst_ref=table_ref.at[slot],
+            send_sem=out_sem,
+            recv_sem=in_sem.at[slot],
+            device_id=peer,
+            device_id_type=MESH,
+        ).start()
+
+    def arrived(slot):
+        pltpu.make_async_copy(table_ref.at[slot], table_ref.at[slot], in_sem.at[slot]).wait()
+
+    def query_arrived(slot):
+        pltpu.make_async_copy(all_ref.at[slot], all_ref.at[slot], query_in_sem.at[slot]).wait()
+
+    def pick(target):
+        def some(step, carry):
+            base = pl.multiple_of(step * 16, 16)
+            for k in range(16):
+                row = wanted_ref[target * per_range + base + k]
+                picked[target, pl.ds(base + k, 1), :] = rows_ref[pl.ds(row, 1), :]
+            return carry
+
+        lax.fori_loop(0, per_range // 16, some, 0)
+
+    def give(step, carry):
+        target = (own + step) % pass_count
+        pick(target)
+        send(picked.at[target], cent * pass_count + own, (cent, target))
         return carry
 
-    lax.fori_loop(0, count // 16, some, 0)
-
-
-def pick_rows(centroids, wanted):
-    count = wanted.shape[0]
+    lax.fori_loop(1, pass_count, give, 0)
+    all_ref[cent] = queries_ref[...]
+    for side in sides:
+        send_query(cent, side)
+    send_query(cent, twin)
+    pick(own)
+    table_ref[cent * pass_count + own] = picked[own]
+
+    def forward(slot):
+        for side in sides:
+            send(table_ref.at[slot], slot, side)
+        send(table_ref.at[slot], slot, twin)
+
+    forward(cent * pass_count + own)
+
+    def take(step, carry):
+        slot = cent * pass_count + (own + pass_count - step) % pass_count
+        arrived(slot)
+        forward(slot)
+        return carry
+
+    lax.fori_loop(1, pass_count, take, 0)
+    for s in range(1, pairs):
+        other = (pair + pairs - s) % pairs * 2 + core
+        query_arrived(other)
+        send_query(other, twin)
+
+        def cross(step, carry):
+            slot = other * pass_count + (own + pass_count - step) % pass_count
+            arrived(slot)
+            send(table_ref.at[slot], slot, twin)
+            return carry
+
+        lax.fori_loop(0, pass_count, cross, 0)
+
+    for k in range(pairs):
+        other = k * 2 + 1 - core
+        query_arrived(other)
+
+        def last(step, carry):
+            arrived(other * pass_count + step)
+            return carry
+
+        lax.fori_loop(0, pass_count, last, 0)
+    sent = table_ref.at[pl.ds(0, cent_count * pass_count - 1)]
+    pltpu.make_async_copy(sent, sent, out_sem).wait()
+    sent = all_ref.at[pl.ds(0, cent_count - 1)]
+    pltpu.make_async_copy(sent, sent, query_out_sem).wait()
+
+
+def spread_rows(queries, centroids, wanted, cent_count, pass_count):
+    per_range = wanted.shape[0] // pass_count
     width = centroids.shape[1]
+    slots = cent_count * pass_count
     return pl.pallas_call(
-        functools.partial(pick_kernel, count),
-        out_shape=jax.ShapeDtypeStruct((count, width), jnp.float32),
+        functools.partial(spread_kernel, pass_count, cent_count, per_range),
+        out_shape=(
+            jax.ShapeDtypeStruct((slots, per_range, width), jnp.float32),
+            jax.ShapeDtypeStruct((cent_count,) + queries.shape, jnp.float32),
+        ),
         in_specs=[
             pl.BlockSpec(memory_space=pltpu.SMEM),
             pl.BlockSpec(memory_space=pltpu.VMEM),
+            pl.BlockSpec(memory_space=pltpu.VMEM),
         ],
-        out_specs=pl.BlockSpec(memory_space=pltpu.VMEM),
-        compiler_params=pltpu.CompilerParams(vmem_limit_bytes=24 * 2**20),
-    )(wanted, centroids)
+        out_specs=(pl.BlockSpec(memory_space=pltpu.VMEM), pl.BlockSpec(memory_space=pltpu.VMEM)),
+        scratch_shapes=[
+            pltpu.VMEM((pass_count, per_range, width), jnp.float32),
+            pltpu.SemaphoreType.DMA,
+            pltpu.SemaphoreType.DMA((slots,)),
+            pltpu.SemaphoreType.DMA,
+            pltpu.SemaphoreType.DMA((cent_count,)),
+        ],
+        compiler_params=pltpu.CompilerParams(
+            collective_id=0, has_side_effects=True, vmem_limit_bytes=40 * 2**20
+        ),
+    )(wanted, centroids, queries)
+
+
+def finish_kernel(
+    pass_count, cent_count, keep, part_ref, mask_ref, every_ref, top_ref, box, out_sem, in_sem, box_out_sem, box_in_sem
+):
+    cent, own = lax.axis_index("cent"), lax.axis_index("pass")
+    group = part_ref.shape[1]
+    across = [(cent + s) % cent_count for s in range(1, cent_count)]
+    along = [(own + s) % pass_count for s in range(1, pass_count)]
+    meet([(c, own) for c in across] + [(cent, p) for p in along])
+    copies = []
+    for k, c in enumerate(across):
+        copy = pltpu.make_async_remote_copy(
+            src_ref=part_ref.at[c],
+            dst_ref=every_ref.at[cent],
+            send_sem=out_sem.at[k],
+            recv_sem=in_sem.at[k],
+            device_id=(c, own),
+            device_id_type=MESH,
+        )
+        copy.start()
+        copies.append(copy)
+    every_ref[cent] = part_ref[cent]
+    for copy in copies:
+        copy.wait()
+    box[own] = jnp.where(mask_ref[...] > 0, every_ref[...], floor_value)
+    copies = []
+    for k, p in enumerate(along):
+        copy = pltpu.make_async_remote_copy(
+            src_ref=box.at[own],
+            dst_ref=box.at[own],
+            send_sem=box_out_sem.at[k],
+            recv_sem=box_in_sem.at[k],
+            device_id=(cent, p),
+            device_id_type=MESH,
+        )
+        copy.start()
+        copies.append(copy)
+    for copy in copies:
+        copy.wait()
+    place = lax.broadcasted_iota(jnp.int32, (group, keep), 1).astype(jnp.float32)
+
+    def step(i, carry):
+        bound, done, top = carry
+        x = box[...]
+        x = x.reshape((pass_count * cent_count,) + x.shape[2:])
+        lower = jnp.max(jnp.where(x < bound, x, -jnp.inf), axis=0)
+        value = jnp.max(lower, axis=1, keepdims=True)
+        same = jnp.sum(jnp.where(x == value, 1.0, 0.0), axis=0)
+        after = done + jnp.sum(same, axis=1, keepdims=True)
+        top = jnp.where((place >= done) & (place < after), value, top)
+        return value, after, top
+
+    first = (
+        jnp.full((group, 1), jnp.inf, jnp.float32),
+        jnp.zeros((group, 1), jnp.float32),
+        jnp.zeros((group, keep), jnp.float32),
+    )
+    top_ref[...] = lax.fori_loop(0, keep, step, first)[2]
+
+
+def finish(parts, mask, pass_count):
+    cent_count, group, mine = parts.shape
+    return pl.pallas_call(
+        functools.partial(finish_kernel, pass_count, cent_count, KTOP),
+        out_shape=(
+            jax.ShapeDtypeStruct(parts.shape, jnp.float32),
+            jax.ShapeDtypeStruct((group, KTOP), jnp.float32),
+        ),
+        in_specs=[pl.BlockSpec(memory_space=pltpu.VMEM)] * 2,
+        out_specs=(pl.BlockSpec(memory_space=pltpu.VMEM), pl.BlockSpec(memory_space=pltpu.VMEM)),
+        scratch_shapes=[
+            pltpu.VMEM((pass_count, cent_count, group, mine), jnp.float32),
+            pltpu.SemaphoreType.DMA((cent_count,)),
+            pltpu.SemaphoreType.DMA((cent_count,)),
+            pltpu.SemaphoreType.DMA((pass_count,)),
+            pltpu.SemaphoreType.DMA((pass_count,)),
+        ],
+        compiler_params=pltpu.CompilerParams(collective_id=1, has_side_effects=True),
+    )(parts, mask)
 
 
 def score_kernel(
@@ -127,16 +334,6 @@
     )(where, codes, bits, weights, both, fold, table)
 
 
-def largest(values, keep):
-    count = values.shape[1]
-    place = jnp.arange(count, dtype=jnp.int32)
-    one, other = values[:, :, None], values[:, None, :]
-    ahead = (other > one) | ((other == one) & (place[None, None, :] < place[None, :, None]))
-    rank = jnp.sum(ahead.astype(jnp.int32), axis=2)
-    hit = rank[:, None, :] == jnp.arange(keep, dtype=jnp.int32)[None, :, None]
-    return jnp.sum(jnp.where(hit, values[:, None, :], 0.0), axis=2)
-
-
 def body(
     queries,
     centroids,
@@ -155,12 +352,9 @@
     per_range = touched.shape[1] // (pass_count * cent_count)
     owner = cent * pass_count + lax.axis_index("pass")
     wanted = lax.dynamic_slice_in_dim(touched, owner * per_range, per_range, 1) - owner * row_count
-    picked = pick_rows(centroids, wanted.reshape(-1))
-    all_queries = lax.all_gather(queries, "cent", axis=0, tiled=True)
-    arrived = lax.all_to_all(
-        picked.reshape(pass_count, per_range, width), "pass", split_axis=0, concat_axis=0, tiled=True
-    )
-    table = lax.all_gather(arrived, "cent", axis=0, tiled=True).reshape(-1, width)
+    table, all_queries = spread_rows(queries, centroids, wanted.reshape(-1), cent_count, pass_count)
+    table = table.reshape(-1, width)
+    all_queries = all_queries.reshape(-1, query_len, width)
 
     passages, passage_len = token_codes.shape
     mine = passages // cent_count
@@ -169,20 +363,20 @@
     scored = score_passages(
         all_queries, table, codes, residual_bits, bucket_weights, cent.reshape(1), mine
     )
-    every = lax.all_to_all(scored.T, "cent", split_axis=0, concat_axis=1, tiled=True)
 
     blocks = candidate_blocks[:, 0, :]
     block_count = blocks.shape[1]
     stored = passages // BLK
-    by_block = every.reshape(group_queries, 1, stored, BLK)
-    chosen = blocks[:, :, None, None] == jnp.arange(stored, dtype=jnp.int32)[None, None, :, None]
-    slots = jnp.sum(jnp.where(chosen, by_block, 0.0), axis=2)
-    live = jnp.arange(block_count, dtype=jnp.int32)[None, :, None] < block_counts[:, :, None]
-    plain = jnp.where(live, slots, 0.0).reshape(group_queries, -1)
-    masked = jnp.where(live, slots, floor_value).reshape(group_queries, -1)
-    local_top = largest(masked, KTOP)
-    every_top = lax.all_gather(local_top, "pass", axis=1, tiled=True)
-    return plain[:, None, :], largest(every_top, KTOP)
+    live = jnp.arange(block_count, dtype=jnp.int32)[None, :] < block_counts
+    holds = blocks[:, :, None] == jnp.arange(stored, dtype=jnp.int32)[None, None, :]
+    wanted_blocks = jnp.any(holds & live[:, :, None], axis=1).astype(jnp.int32)
+    mask = jnp.repeat(wanted_blocks, BLK, axis=1).reshape(group_queries, cent_count, mine)
+    parts = scored.T.reshape(cent_count, group_queries, mine)
+    every, top = finish(parts, mask.transpose(1, 0, 2), pass_count)
+    by_block = every.transpose(1, 0, 2).reshape(group_queries, 1, stored, BLK)
+    slots = jnp.sum(jnp.where(holds[:, :, :, None], by_block, 0.0), axis=2)
+    plain = jnp.where(live[:, :, None], slots, 0.0).reshape(group_queries, -1)
+    return plain[:, None, :], top
 
 
 def solution(mesh):

time: 127 us -> 72.8 us (0.57)
  blocking collectives: 59.5 us -> 0 us
  Pallas kernels: 19.8 us -> 61.5 us
  waiting for transfers between devices: 17.1 us -> 0 us
  between operations: 14.3 us -> 0.83 us
  other arithmetic: 6.08 us -> 2 us
  starting transfers between devices: 3.29 us -> 0 us
  local copies, waits for them, and re-layouts: 6.15 us -> 8.05 us
    pallas_call x1 -> x2, Pallas kernels: 1.68 us -> 43.3 us  [the longest x1 25.7 us: spread_rows(): pl.pallas_call(functools.partial(spread_kernel, pass_count, cent_count, p...]
    all_gather x2 -> x0, blocking collectives: 37.7 us -> none  [the longest x1 30.5 us: body(): every_top = lax.all_gather(local_top, 'pass', axis=1, tiled=True)]
    all_to_all x1 -> x0, blocking collectives: 21.8 us -> none  [body(): lax.all_to_all(picked.reshape(pass_count, per_range, width), 'pass', spli...]
    all_gather x1 -> x0, waiting for transfers between devices: 13.3 us -> none  [body(): lax.all_gather(arrived, 'cent', axis=0, tiled=True).reshape(-1, width)]
    reduce_sum x5 -> x1, other arithmetic: 4.69 us -> 0.63 us  [body(): slots = jnp.sum(jnp.where(holds[:, :, :, None], by_block, 0.0), axis=2)]
    all_to_all x1 -> x0, waiting for transfers between devices: 3.79 us -> none  [body(): lax.all_to_all(scored.T, 'cent', split_axis=0, concat_axis=1, tiled=True)]
    all_to_all x1 -> x0, starting transfers between devices: 3.25 us -> none  [body(): lax.all_to_all(scored.T, 'cent', split_axis=0, concat_axis=1, tiled=True)]
    unnamed x16 -> x14, local copies, waits for them, and re-layouts: 3.98 us -> 4.48 us
  transfers between devices with their start and end apart: 2 -> 0, of which waited for: 2 -> 0; matrix products, arithmetic and copies ran while one was open for 1% -> 0% of each run, Pallas kernels for 0% -> 0%
where the time goes in v2:
time: 72.8 us; the launch traced here: 72.3 us
  Pallas kernels  61.5 us (84%)
  local copies, waits for them, and re-layouts  8.05 us (11%)
  other arithmetic  2 us (3%)
  between operations  0.83 us (1%)
    pallas_call x1, Pallas kernels, spread_rows(): pl.pallas_call(functools.partial(spread_kernel, pass_count, cent_count, p...  25.7 us
    pallas_call x1, Pallas kernels, score_passages(): pl.pallas_call(functools.partial(score_kernel, passage_len), out_shape=ja...  18.2 us
    pallas_call x1, Pallas kernels, finish(): pl.pallas_call(functools.partial(finish_kernel, pass_count, cent_count, K...  17.6 us
    unnamed x14, local copies, waits for them, and re-layouts  4.48 us

profile of v2, /device:TPU:0, one launch (start us, length us, event | category | flops | bytes accessed | tf_op | source)
XLA Modules:
  0.0 72.3 jit_solution(215209341228629899)
XLA Ops:
  0.7 0.7 %subtract_bitcast_fusion.wanted_ref = s32[1024]{0:T(1024)S(1)} fusion(s32[8,4096]{1,0:T(8,128)} %param.11, s32[]{:T(128)S(6)} %select_n.35, s32[]{:T(128)S(6)} %mul.15), kind=kLoop, calls=%fused_computation.17 | loop fusion | flops 1024 | bytes 8200 | tf_op jit(solution)/shard_map/reshape | solution.py:355
  1.4 2.2 %copy-done.1 = f32[8192,128]{1,0:T(8,128)S(1)} copy-done((f32[8192,128]{1,0:T(8,128)S(1)}, f32[8192,128]{1,0:T(8,128)}, u32[]{:S(2)}) %copy-start.1) | copy-done | bytes 4194328
  3.6 0.9 %copy-done.2 = f32[8,32,128]{2,1,0:T(8,128)S(1)} copy-done((f32[8,32,128]{2,1,0:T(8,128)S(1)}, f32[8,32,128]{2,1,0:T(8,128)}, u32[]{:S(2)}) %copy-start.2) | copy-done | bytes 131096
  4.5 25.7 %shard_map.98 = (f32[32,128,128]{2,1,0:T(8,128)S(1)}, f32[4,8,32,128]{3,2,1,0:T(8,128)S(1)}) custom-call(s32[1024]{0:T(1024)S(1)} %subtract_bitcast_fusion.wanted_ref, f32[8192,128]{1,0:T(8,128)S(1)} %copy-done.1, f32[8,32,128]{2,1,0:T(8,128)S(1)} %copy-done.2), custom_call_target="tpu_custom_call" | custom-call | tf_op jit(solution)/shard_map/pallas_call | solution.py:145
  30.2 0.2 copy.22
  30.4 0.1 reduce-precision_convert_fusion
  30.5 0.1 copy.29
  30.6 0.1 copy.21
  30.8 0.1 reshape.110.codes_ref
  30.9 0.2 fusion.1.fold_ref
  31.2 18.2 %shard_map.99 = f32[128,32]{1,0:T(8,128)S(1)} custom-call(s32[1]{0:T(128)} %bitcast.2.where_ref, s32[8192]{0:T(1024)S(1)} %reshape.110.codes_ref, s32[512,2048]{1,0:T(8,128)} %bits_ref.1, f32[4,128]{1,0:T(4,128)S(1)} %copy-done.3, bf16[256,1024]{1,0:T(8,128)(2,1)S(1)} %maximum_bitcast_fusion.query_ref, f32[1024,32]{1,0:T(8,128)S(1)} %fusion.1.fold_ref, ...), custom_call_target="tpu_custom_call" | custom-call | tf_op jit(solution)/shard_map/pallas_call | solution.py:317
  49.3 0.7 copy.24
  50.1 0.1 iota_compare_fusion.1
  50.3 0.1 broadcast_in_dim.46
  50.4 0.1 reshape_reshape.7
  50.5 0.6 copy.31
  51.1 17.6 %shard_map.100 = (f32[4,8,128]{2,1,0:T(8,128)}, f32[8,32]{1,0:T(8,128)}) custom-call(f32[4,8,128]{2,1,0:T(8,128)} %bitcast.22, s32[4,8,128]{2,1,0:T(8,128)} %bitcast.23), custom_call_target="tpu_custom_call" | custom-call | tf_op jit(solution)/shard_map/pallas_call | solution.py:231
  68.7 0.7 copy.26
  69.4 0.1 broadcast_in_dim.47
  69.5 0.1 copy.27
  69.6 0.6 select_reduce_fusion
  70.2 0.1 broadcast_select_fusion
  70.4 0.7 select_n.40
  71.1 1.3 %copy.33 = f32[8,32]{1,0:T(8,128)} copy(f32[8,32]{1,0:T(8,128)} %get-tuple-element.21) | data formatting | bytes 2048
  (15 shorter events, 0.2 us)
Async XLA Ops:
  0.6 29.9 %copy-start = (s32[512,64]{0,1:T(8,128)S(1)}, s32[512,64]{0,1:T(8,128)}, u32[]{:S(2)}) copy-start(s32[512,64]{0,1:T(8,128)} %param.12) | copy-start | bytes 393220
  1.4 2.2 %copy-start.1 = (f32[8192,128]{1,0:T(8,128)S(1)}, f32[8192,128]{1,0:T(8,128)}, u32[]{:S(2)}) copy-start(f32[8192,128]{1,0:T(8,128)} %rows_ref.1) | copy-start | bytes 12582916
  3.6 0.9 %copy-start.2 = (f32[8,32,128]{2,1,0:T(8,128)S(1)}, f32[8,32,128]{2,1,0:T(8,128)}, u32[]{:S(2)}) copy-start(f32[8,32,128]{2,1,0:T(8,128)} %queries_ref.1) | copy-start | bytes 393220
  30.2 1.0 %copy-start.3 = (f32[4,128]{1,0:T(4,128)S(1)}, f32[4,128]{1,0:T(4,128)}, u32[]{:S(2)}) copy-start(f32[4,128]{1,0:T(4,128)} %weights_ref.1) | copy-start | bytes 6148
  31.1 18.9 %copy-start.5 = (s32[8,1]{0,1:T(1,128)S(1)}, s32[8,1]{0,1:T(1,128)}, u32[]{:S(2)}) copy-start(s32[8,1]{0,1:T(1,128)} %param.15) | copy-start | bytes 100
  31.1 19.0 %copy-start.4 = (s32[8,1,32]{2,1,0:T(1,128)S(1)}, s32[8,1,32]{2,1,0:T(1,128)}, u32[]{:S(2)}) copy-start(s32[8,1,32]{2,1,0:T(1,128)} %param.14) | copy-start | bytes 3076

commit v3 on v2

--- a/solution.py
+++ b/solution.py
@@ -168,10 +168,9 @@
 
 
 def finish_kernel(
-    pass_count, cent_count, keep, part_ref, mask_ref, every_ref, top_ref, box, out_sem, in_sem, box_out_sem, box_in_sem
+    pass_count, cent_count, part_ref, mask_ref, every_ref, box, out_sem, in_sem, box_out_sem, box_in_sem
 ):
     cent, own = lax.axis_index("cent"), lax.axis_index("pass")
-    group = part_ref.shape[1]
     across = [(cent + s) % cent_count for s in range(1, cent_count)]
     along = [(own + s) % pass_count for s in range(1, pass_count)]
     meet([(c, own) for c in across] + [(cent, p) for p in along])
@@ -205,39 +204,75 @@
         copies.append(copy)
     for copy in copies:
         copy.wait()
-    place = lax.broadcasted_iota(jnp.int32, (group, keep), 1).astype(jnp.float32)
-
-    def step(i, carry):
-        bound, done, top = carry
-        x = box[...]
-        x = x.reshape((pass_count * cent_count,) + x.shape[2:])
-        lower = jnp.max(jnp.where(x < bound, x, -jnp.inf), axis=0)
-        value = jnp.max(lower, axis=1, keepdims=True)
-        same = jnp.sum(jnp.where(x == value, 1.0, 0.0), axis=0)
-        after = done + jnp.sum(same, axis=1, keepdims=True)
-        top = jnp.where((place >= done) & (place < after), value, top)
-        return value, after, top
-
-    first = (
-        jnp.full((group, 1), jnp.inf, jnp.float32),
-        jnp.zeros((group, 1), jnp.float32),
-        jnp.zeros((group, keep), jnp.float32),
-    )
-    top_ref[...] = lax.fori_loop(0, keep, step, first)[2]
+
+
+def exchange(values, near, far):
+    return jnp.maximum(values[near], values[far]), jnp.minimum(values[near], values[far])
+
+
+def settle(values):
+    gap = len(values) // 2
+    while gap:
+        for i in range(len(values)):
+            if not i & gap:
+                values[i], values[i + gap] = exchange(values, i, i + gap)
+        gap //= 2
+    return values
+
+
+def descending(values):
+    if len(values) == 1:
+        return values
+    half = len(values) // 2
+    return settle(descending(values[:half]) + descending(values[half:])[::-1])
+
+
+def merged(first, second):
+    return settle([jnp.maximum(x, y) for x, y in zip(first, second[::-1])])
+
+
+def top_kernel(keep, box_ref, top_ref):
+    pass_count, cent_count, group, mine = box_ref.shape
+    values = [box_ref[p, c] for p in range(pass_count) for c in range(cent_count)]
+    runs = [descending(values[i : i + keep]) for i in range(0, len(values), keep)]
+    best = runs[0]
+    for run in runs[1:]:
+        best = merged(best, run)
+    gap = mine // 2
+    while gap:
+        if mine % 128 == 0:
+            moved = [pltpu.roll(x, gap, 1) for x in best]
+        else:
+            moved = [jnp.concatenate([x[:, gap:], x[:, :gap]], axis=1) for x in best]
+        best = merged(best, moved)
+        gap //= 2
+    place = lax.broadcasted_iota(jnp.int32, (group, mine), 1)
+    out = best[0]
+    for k in range(1, keep):
+        out = jnp.where(place == k, best[k], out)
+    top_ref[...] = out[:, :keep]
+
+
+def largest(box):
+    return pl.pallas_call(
+        functools.partial(top_kernel, KTOP),
+        out_shape=jax.ShapeDtypeStruct((box.shape[2], KTOP), jnp.float32),
+        in_specs=[pl.BlockSpec(memory_space=pltpu.VMEM)],
+        out_specs=pl.BlockSpec(memory_space=pltpu.VMEM),
+    )(box)
 
 
 def finish(parts, mask, pass_count):
-    cent_count, group, mine = parts.shape
+    cent_count = parts.shape[0]
     return pl.pallas_call(
-        functools.partial(finish_kernel, pass_count, cent_count, KTOP),
+        functools.partial(finish_kernel, pass_count, cent_count),
         out_shape=(
             jax.ShapeDtypeStruct(parts.shape, jnp.float32),
-            jax.ShapeDtypeStruct((group, KTOP), jnp.float32),
+            jax.ShapeDtypeStruct((pass_count,) + parts.shape, jnp.float32),
         ),
         in_specs=[pl.BlockSpec(memory_space=pltpu.VMEM)] * 2,
         out_specs=(pl.BlockSpec(memory_space=pltpu.VMEM), pl.BlockSpec(memory_space=pltpu.VMEM)),
         scratch_shapes=[
-            pltpu.VMEM((pass_count, cent_count, group, mine), jnp.float32),
             pltpu.SemaphoreType.DMA((cent_count,)),
             pltpu.SemaphoreType.DMA((cent_count,)),
             pltpu.SemaphoreType.DMA((pass_count,)),
@@ -248,7 +283,7 @@
 
 
 def score_kernel(
-    passage_len, where_ref, codes_ref, bits_ref, weights_ref, query_ref, fold_ref, table_ref, out_ref, held
+    passage_len, where_ref, codes_ref, bits_ref, weights_ref, query_ref, fold_ref, table_ref, out_ref, held, best
 ):
     chunk = pl.program_id(0)
     width = weights_ref.shape[1]
@@ -293,14 +328,18 @@
     token = (held[...] + residual).astype(jnp.bfloat16)
     token = jnp.concatenate([token, token], axis=1)
     score = jnp.dot(token, query_ref[...], preferred_element_type=jnp.float32)
-    best = jnp.max(score.reshape(passage_len, CHUNK, score.shape[1]), axis=0)
-    out_ref[...] = lax.dot_general(
-        best,
-        fold_ref[...],
-        (((1,), (0,)), ((), ())),
-        precision=lax.Precision.HIGHEST,
-        preferred_element_type=jnp.float32,
-    )
+    peak = jnp.max(score.reshape(passage_len, CHUNK, score.shape[1]), axis=0)
+    best[pl.ds(pl.multiple_of(chunk * CHUNK, CHUNK), CHUNK), :] = peak
+
+    @pl.when(chunk == pl.num_programs(0) - 1)
+    def _():
+        out_ref[...] = lax.dot_general(
+            fold_ref[...],
+            best[...],
+            (((1,), (1,)), ((), ())),
+            precision=lax.Precision.HIGHEST,
+            preferred_element_type=jnp.float32,
+        )
 
 
 def score_passages(all_queries, table, codes, bits, weights, where, mine):
@@ -310,13 +349,13 @@
     high = lax.reduce_precision(flat, 8, 7)
     both = jnp.concatenate([high, flat - high], axis=1).T.astype(jnp.bfloat16)
     fold = (
-        jnp.arange(query_count * query_len)[:, None] // query_len == jnp.arange(query_count)[None, :]
+        jnp.arange(query_count * query_len)[None, :] // query_len == jnp.arange(query_count)[:, None]
     ).astype(jnp.float32)
     chunks = mine // CHUNK
     whole = pl.Buffered(buffer_count=1)
     return pl.pallas_call(
         functools.partial(score_kernel, passage_len),
-        out_shape=jax.ShapeDtypeStruct((mine, query_count), jnp.float32),
+        out_shape=jax.ShapeDtypeStruct((query_count, mine), jnp.float32),
         grid_spec=pltpu.PrefetchScalarGridSpec(
             num_scalar_prefetch=2,
             grid=(chunks,),
@@ -327,8 +366,11 @@
                 pl.BlockSpec(fold.shape, lambda c, w, k: (0, 0), pipeline_mode=whole),
                 pl.BlockSpec(table.shape, lambda c, w, k: (0, 0), pipeline_mode=whole),
             ],
-            out_specs=pl.BlockSpec((CHUNK, query_count), lambda c, w, k: (c, 0)),
-            scratch_shapes=[pltpu.VMEM((passage_len * CHUNK, width), jnp.float32)],
+            out_specs=pl.BlockSpec((query_count, mine), lambda c, w, k: (0, 0)),
+            scratch_shapes=[
+                pltpu.VMEM((passage_len * CHUNK, width), jnp.float32),
+                pltpu.VMEM((mine, query_count * query_len), jnp.float32),
+            ],
         ),
         compiler_params=pltpu.CompilerParams(vmem_limit_bytes=48 * 2**20),
     )(where, codes, bits, weights, both, fold, table)
@@ -371,12 +413,12 @@
     holds = blocks[:, :, None] == jnp.arange(stored, dtype=jnp.int32)[None, None, :]
     wanted_blocks = jnp.any(holds & live[:, :, None], axis=1).astype(jnp.int32)
     mask = jnp.repeat(wanted_blocks, BLK, axis=1).reshape(group_queries, cent_count, mine)
-    parts = scored.T.reshape(cent_count, group_queries, mine)
-    every, top = finish(parts, mask.transpose(1, 0, 2), pass_count)
+    parts = scored.reshape(cent_count, group_queries, mine)
+    every, box = finish(parts, mask.transpose(1, 0, 2), pass_count)
     by_block = every.transpose(1, 0, 2).reshape(group_queries, 1, stored, BLK)
     slots = jnp.sum(jnp.where(holds[:, :, :, None], by_block, 0.0), axis=2)
     plain = jnp.where(live[:, :, None], slots, 0.0).reshape(group_queries, -1)
-    return plain[:, None, :], top
+    return plain[:, None, :], largest(box)
 
 
 def solution(mesh):

time: 72.8 us -> 65.5 us (0.90)
  Pallas kernels: 61.5 us -> 55.6 us
  local copies, waits for them, and re-layouts: 8.05 us -> 6.71 us
    pallas_call x1 -> x2, Pallas kernels: 17.6 us -> 13.4 us  [the longest x1 11.1 us: finish(): pl.pallas_call(functools.partial(finish_kernel, pass_count, cent_count),...]
    pallas_call x1, Pallas kernels: 18.2 us -> 16.6 us  [score_passages(): pl.pallas_call(functools.partial(score_kernel, passage_len), out_shape=ja...]
    unnamed x14 -> x15, local copies, waits for them, and re-layouts: 4.48 us -> 3.81 us
where the time goes in v3:
time: 65.5 us; the launch traced here: 65 us
  Pallas kernels  55.6 us (85%)
  local copies, waits for them, and re-layouts  6.71 us (10%)
  other arithmetic  1.81 us (3%)
  between operations  0.84 us (1%)
    pallas_call x1, Pallas kernels, spread_rows(): pl.pallas_call(functools.partial(spread_kernel, pass_count, cent_count, p...  25.7 us
    pallas_call x1, Pallas kernels, score_passages(): pl.pallas_call(functools.partial(score_kernel, passage_len), out_shape=ja...  16.6 us
    pallas_call x1, Pallas kernels, finish(): pl.pallas_call(functools.partial(finish_kernel, pass_count, cent_count),...  11.1 us
    unnamed x15, local copies, waits for them, and re-layouts  3.81 us
    pallas_call x1, Pallas kernels, largest(): pl.pallas_call(functools.partial(top_kernel, KTOP), out_shape=jax.ShapeDt...  2.31 us

profile of v3, /device:TPU:0, one launch (start us, length us, event | category | flops | bytes accessed | tf_op | source)
XLA Modules:
  0.0 65.0 jit_solution(9015554011687442402)
XLA Ops:
  0.7 0.7 %subtract_bitcast_fusion.wanted_ref = s32[1024]{0:T(1024)S(1)} fusion(s32[8,4096]{1,0:T(8,128)} %param.11, s32[]{:T(128)S(6)} %select_n.35, s32[]{:T(128)S(6)} %mul.15), kind=kLoop, calls=%fused_computation.17 | loop fusion | flops 1024 | bytes 8200 | tf_op jit(solution)/shard_map/reshape | solution.py:397
  1.4 2.2 %copy-done.1 = f32[8192,128]{1,0:T(8,128)S(1)} copy-done((f32[8192,128]{1,0:T(8,128)S(1)}, f32[8192,128]{1,0:T(8,128)}, u32[]{:S(2)}) %copy-start.1) | copy-done | bytes 4194328
  3.6 0.9 %copy-done.2 = f32[8,32,128]{2,1,0:T(8,128)S(1)} copy-done((f32[8,32,128]{2,1,0:T(8,128)S(1)}, f32[8,32,128]{2,1,0:T(8,128)}, u32[]{:S(2)}) %copy-start.2) | copy-done | bytes 131096
  4.5 25.7 %shard_map.98 = (f32[32,128,128]{2,1,0:T(8,128)S(1)}, f32[4,8,32,128]{3,2,1,0:T(8,128)S(1)}) custom-call(s32[1024]{0:T(1024)S(1)} %subtract_bitcast_fusion.wanted_ref, f32[8192,128]{1,0:T(8,128)S(1)} %copy-done.1, f32[8,32,128]{2,1,0:T(8,128)S(1)} %copy-done.2), custom_call_target="tpu_custom_call" | custom-call | tf_op jit(solution)/shard_map/pallas_call | solution.py:145
  30.2 0.2 copy.20
  30.4 0.1 reduce-precision_convert_fusion
  30.5 0.1 copy.26
  30.6 0.1 copy.19
  30.8 0.1 reshape.110.codes_ref
  31.0 16.6 %shard_map.99 = f32[32,128]{1,0:T(8,128)S(1)} custom-call(s32[1]{0:T(128)} %bitcast.2.where_ref, s32[8192]{0:T(1024)S(1)} %reshape.110.codes_ref, s32[512,2048]{1,0:T(8,128)} %bits_ref.1, f32[4,128]{1,0:T(4,128)S(1)} %copy-done.4, bf16[256,1024]{1,0:T(8,128)(2,1)S(1)} %maximum_bitcast_fusion.query_ref, f32[32,1024]{1,0:T(8,128)S(1)} %fusion.1.fold_ref, ...), custom_call_target="tpu_custom_call" | custom-call | tf_op jit(solution)/shard_map/pallas_call | solution.py:356
  47.6 0.6 copy-done.3
  48.2 0.1 iota_compare_fusion.2
  48.2 0.1 iota_compare_fusion.1
  48.4 0.1 broadcast_in_dim.46
  48.5 0.1 reshape_reshape.7
  48.6 0.6 copy.28
  49.2 11.1 %shard_map.100 = (f32[4,8,128]{2,1,0:T(8,128)}, f32[8,4,8,128]{3,2,1,0:T(8,128)}) custom-call(f32[4,8,128]{2,1,0:T(8,128)} %bitcast.19, s32[4,8,128]{2,1,0:T(8,128)} %bitcast.21), custom_call_target="tpu_custom_call" | custom-call | tf_op jit(solution)/shard_map/pallas_call | solution.py:267
  60.3 0.7 %copy.23 = f32[8,4,128]{2,1,0:T(4,128)S(1)} copy(f32[8,4,128]{2,0,1:T(8,128)} %bitcast.22) | data formatting | bytes 32768 | tf_op jit(solution)/shard_map/transpose | solution.py:418
  61.0 0.1 broadcast_in_dim.47
  61.1 0.1 copy.24
  61.2 0.6 select_reduce_fusion
  61.9 0.1 broadcast_select_fusion
  62.0 0.7 %select_n.40 = f32[8,1,512]{2,1,0:T(1,128)} reshape(f32[8,32,16]{2,1,0:T(8,128)S(1)} %broadcast_select_fusion) | data formatting | bytes 32768 | tf_op jit(solution)/shard_map/jit(_where)/select_n | solution.py:420
  62.7 2.3 %shard_map.101 = f32[8,32]{1,0:T(8,128)} custom-call(f32[8,4,8,128]{3,2,1,0:T(8,128)} %get-tuple-element.9.box_ref), custom_call_target="tpu_custom_call" | custom-call | tf_op jit(solution)/shard_map/pallas_call | solution.py:257
  (16 shorter events, 0.1 us)
Async XLA Ops:
  0.6 29.9 %copy-start = (s32[512,64]{0,1:T(8,128)S(1)}, s32[512,64]{0,1:T(8,128)}, u32[]{:S(2)}) copy-start(s32[512,64]{0,1:T(8,128)} %param.12) | copy-start | bytes 393220
  1.4 2.2 %copy-start.1 = (f32[8192,128]{1,0:T(8,128)S(1)}, f32[8192,128]{1,0:T(8,128)}, u32[]{:S(2)}) copy-start(f32[8192,128]{1,0:T(8,128)} %rows_ref.1) | copy-start | bytes 12582916
  3.6 0.9 %copy-start.2 = (f32[8,32,128]{2,1,0:T(8,128)S(1)}, f32[8,32,128]{2,1,0:T(8,128)}, u32[]{:S(2)}) copy-start(f32[8,32,128]{2,1,0:T(8,128)} %queries_ref.1) | copy-start | bytes 393220
  30.2 0.8 %copy-start.4 = (f32[4,128]{1,0:T(4,128)S(1)}, f32[4,128]{1,0:T(4,128)}, u32[]{:S(2)}) copy-start(f32[4,128]{1,0:T(4,128)} %weights_ref.1) | copy-start | bytes 6148
  30.9 17.2 %copy-start.6 = (s32[8,1]{0,1:T(1,128)S(1)}, s32[8,1]{0,1:T(1,128)}, u32[]{:S(2)}) copy-start(s32[8,1]{0,1:T(1,128)} %param.15) | copy-start | bytes 100
  31.0 17.3 %copy-start.5 = (s32[8,1,32]{2,1,0:T(1,128)S(1)}, s32[8,1,32]{2,1,0:T(1,128)}, u32[]{:S(2)}) copy-start(s32[8,1,32]{2,1,0:T(1,128)} %param.14) | copy-start | bytes 3076
  47.6 0.6 copy-start.3

commit v4 on v3

--- a/solution.py
+++ b/solution.py
@@ -29,11 +29,13 @@
     cent_count,
     per_range,
     wanted_ref,
-    rows_ref,
+    stored_ref,
     queries_ref,
     table_ref,
     all_ref,
+    rows_ref,
     picked,
+    fetch_sem,
     out_sem,
     in_sem,
     query_out_sem,
@@ -44,7 +46,10 @@
     pairs = cent_count // 2
     twin = (cent + 1 - 2 * core, own)
     sides = [((pair + s) % pairs * 2 + core, own) for s in range(1, pairs)]
+    fetch = pltpu.make_async_copy(stored_ref, rows_ref, fetch_sem)
+    fetch.start()
     meet([(cent, (own + s) % pass_count) for s in range(1, pass_count)] + sides + [twin])
+    fetch.wait()
 
     def send_query(slot, peer, source=None):
         pltpu.make_async_remote_copy(
@@ -150,19 +155,21 @@
         ),
         in_specs=[
             pl.BlockSpec(memory_space=pltpu.SMEM),
-            pl.BlockSpec(memory_space=pltpu.VMEM),
+            pl.BlockSpec(memory_space=pltpu.HBM),
             pl.BlockSpec(memory_space=pltpu.VMEM),
         ],
         out_specs=(pl.BlockSpec(memory_space=pltpu.VMEM), pl.BlockSpec(memory_space=pltpu.VMEM)),
         scratch_shapes=[
+            pltpu.VMEM(centroids.shape, jnp.float32),
             pltpu.VMEM((pass_count, per_range, width), jnp.float32),
+            pltpu.SemaphoreType.DMA,
             pltpu.SemaphoreType.DMA,
             pltpu.SemaphoreType.DMA((slots,)),
             pltpu.SemaphoreType.DMA,
             pltpu.SemaphoreType.DMA((cent_count,)),
         ],
         compiler_params=pltpu.CompilerParams(
-            collective_id=0, has_side_effects=True, vmem_limit_bytes=40 * 2**20
+            collective_id=0, has_side_effects=True, vmem_limit_bytes=51 * 2**20
         ),
     )(wanted, centroids, queries)
 

time: 65.5 us -> 63.3 us (0.966)
  local copies, waits for them, and re-layouts: 6.71 us -> 4.51 us
    unnamed x15 -> x13, local copies, waits for them, and re-layouts: 3.81 us -> 1.62 us
    pallas_call x1, Pallas kernels: 11.1 us -> 11.9 us  [finish(): pl.pallas_call(functools.partial(finish_kernel, pass_count, cent_count),...]
    pallas_call x1, Pallas kernels: 25.7 us -> 24.9 us  [spread_rows(): pl.pallas_call(functools.partial(spread_kernel, pass_count, cent_count, p...]
where the time goes in v4:
time: 63.3 us; the launch traced here: 62.8 us
  Pallas kernels  55.7 us (88%)
  local copies, waits for them, and re-layouts  4.51 us (7%)
  other arithmetic  1.81 us (3%)
  between operations  0.84 us (1%)
    pallas_call x1, Pallas kernels, spread_rows(): pl.pallas_call(functools.partial(spread_kernel, pass_count, cent_count, p...  24.9 us
    pallas_call x1, Pallas kernels, score_passages(): pl.pallas_call(functools.partial(score_kernel, passage_len), out_shape=ja...  16.6 us
    pallas_call x1, Pallas kernels, finish(): pl.pallas_call(functools.partial(finish_kernel, pass_count, cent_count),...  11.9 us
    pallas_call x1, Pallas kernels, largest(): pl.pallas_call(functools.partial(top_kernel, KTOP), out_shape=jax.ShapeDt...  2.31 us
    unnamed x13, local copies, waits for them, and re-layouts  1.62 us

profile of v4, /device:TPU:0, one launch (start us, length us, event | category | flops | bytes accessed | tf_op | source)
XLA Modules:
  0.0 62.8 jit_solution(1902523235252484891)
XLA Ops:
  0.6 0.0 copy-start
  0.7 0.7 %subtract_bitcast_fusion.wanted_ref = s32[1024]{0:T(1024)S(1)} fusion(s32[8,4096]{1,0:T(8,128)} %param.11, s32[]{:T(128)S(6)} %select_n.35, s32[]{:T(128)S(6)} %mul.15), kind=kLoop, calls=%fused_computation.17 | loop fusion | flops 1024 | bytes 8200 | tf_op jit(solution)/shard_map/reshape | solution.py:404
  1.4 0.9 %copy-done.1 = f32[8,32,128]{2,1,0:T(8,128)S(1)} copy-done((f32[8,32,128]{2,1,0:T(8,128)S(1)}, f32[8,32,128]{2,1,0:T(8,128)}, u32[]{:S(2)}) %copy-start.1) | copy-done | bytes 131096
  2.3 24.9 %shard_map.98 = (f32[32,128,128]{2,1,0:T(8,128)S(1)}, f32[4,8,32,128]{3,2,1,0:T(8,128)S(1)}) custom-call(s32[1024]{0:T(1024)S(1)} %subtract_bitcast_fusion.wanted_ref, f32[8192,128]{1,0:T(8,128)} %stored_ref.1, f32[8,32,128]{2,1,0:T(8,128)S(1)} %copy-done.1), custom_call_target="tpu_custom_call" | custom-call | tf_op jit(solution)/shard_map/pallas_call | solution.py:150
  27.2 0.2 copy.20
  27.4 0.1 reduce-precision_convert_fusion
  27.6 0.1 copy.26
  27.7 0.1 copy.19
  27.8 0.1 reshape.110.codes_ref
  28.0 16.6 %shard_map.99 = f32[32,128]{1,0:T(8,128)S(1)} custom-call(s32[1]{0:T(128)} %bitcast.2.where_ref, s32[8192]{0:T(1024)S(1)} %reshape.110.codes_ref, s32[512,2048]{1,0:T(8,128)} %bits_ref.1, f32[4,128]{1,0:T(4,128)S(1)} %copy-done.3, bf16[256,1024]{1,0:T(8,128)(2,1)S(1)} %maximum_bitcast_fusion.query_ref, f32[32,1024]{1,0:T(8,128)S(1)} %fusion.1.fold_ref, ...), custom_call_target="tpu_custom_call" | custom-call | tf_op jit(solution)/shard_map/pallas_call | solution.py:363
  44.6 0.6 copy-done.2
  45.2 0.1 iota_compare_fusion.2
  45.3 0.1 iota_compare_fusion.1
  45.5 0.1 broadcast_in_dim.46
  45.6 0.1 reshape_reshape.7
  45.7 0.6 copy.28
  46.3 11.9 %shard_map.100 = (f32[4,8,128]{2,1,0:T(8,128)}, f32[8,4,8,128]{3,2,1,0:T(8,128)}) custom-call(f32[4,8,128]{2,1,0:T(8,128)} %bitcast.19, s32[4,8,128]{2,1,0:T(8,128)} %bitcast.21), custom_call_target="tpu_custom_call" | custom-call | tf_op jit(solution)/shard_map/pallas_call | solution.py:274
  58.1 0.7 %copy.23 = f32[8,4,128]{2,1,0:T(4,128)S(1)} copy(f32[8,4,128]{2,0,1:T(8,128)} %bitcast.22) | data formatting | bytes 32768 | tf_op jit(solution)/shard_map/transpose | solution.py:425
  58.9 0.1 broadcast_in_dim.47
  59.0 0.1 copy.24
  59.0 0.6 select_reduce_fusion
  59.7 0.1 broadcast_select_fusion
  59.8 0.7 %select_n.40 = f32[8,1,512]{2,1,0:T(1,128)} reshape(f32[8,32,16]{2,1,0:T(8,128)S(1)} %broadcast_select_fusion) | data formatting | bytes 32768 | tf_op jit(solution)/shard_map/jit(_where)/select_n | solution.py:427
  60.5 2.3 %shard_map.101 = f32[8,32]{1,0:T(8,128)} custom-call(f32[8,4,8,128]{3,2,1,0:T(8,128)} %get-tuple-element.9.box_ref), custom_call_target="tpu_custom_call" | custom-call | tf_op jit(solution)/shard_map/pallas_call | solution.py:264
  (14 shorter events, 0.1 us)
Async XLA Ops:
  0.6 26.9 %copy-start = (s32[512,64]{0,1:T(8,128)S(1)}, s32[512,64]{0,1:T(8,128)}, u32[]{:S(2)}) copy-start(s32[512,64]{0,1:T(8,128)} %param.12) | copy-start | bytes 393220
  1.4 0.9 %copy-start.1 = (f32[8,32,128]{2,1,0:T(8,128)S(1)}, f32[8,32,128]{2,1,0:T(8,128)}, u32[]{:S(2)}) copy-start(f32[8,32,128]{2,1,0:T(8,128)} %queries_ref.1) | copy-start | bytes 393220
  27.2 0.8 %copy-start.3 = (f32[4,128]{1,0:T(4,128)S(1)}, f32[4,128]{1,0:T(4,128)}, u32[]{:S(2)}) copy-start(f32[4,128]{1,0:T(4,128)} %weights_ref.1) | copy-start | bytes 6148
  28.0 17.2 %copy-start.5 = (s32[8,1]{0,1:T(1,128)S(1)}, s32[8,1]{0,1:T(1,128)}, u32[]{:S(2)}) copy-start(s32[8,1]{0,1:T(1,128)} %param.15) | copy-start | bytes 100
  28.0 17.3 %copy-start.4 = (s32[8,1,32]{2,1,0:T(1,128)S(1)}, s32[8,1,32]{2,1,0:T(1,128)}, u32[]{:S(2)}) copy-start(s32[8,1,32]{2,1,0:T(1,128)} %param.14) | copy-start | bytes 3076
  44.6 0.6 copy-start.2

commit v5 on v4

--- a/solution.py
+++ b/solution.py
@@ -87,6 +87,15 @@
 
         lax.fori_loop(0, per_range // 16, some, 0)
 
+    def forward(slot):
+        for side in sides:
+            send(table_ref.at[slot], slot, side)
+        send(table_ref.at[slot], slot, twin)
+
+    pick(own)
+    table_ref[cent * pass_count + own] = picked[own]
+    forward(cent * pass_count + own)
+
     def give(step, carry):
         target = (own + step) % pass_count
         pick(target)
@@ -98,15 +107,6 @@
     for side in sides:
         send_query(cent, side)
     send_query(cent, twin)
-    pick(own)
-    table_ref[cent * pass_count + own] = picked[own]
-
-    def forward(slot):
-        for side in sides:
-            send(table_ref.at[slot], slot, side)
-        send(table_ref.at[slot], slot, twin)
-
-    forward(cent * pass_count + own)
 
     def take(step, carry):
         slot = cent * pass_count + (own + pass_count - step) % pass_count

time: 63.3 us -> 63.5 us (level)
  no operation moved by 1% of the time
where the time goes in v5:
time: 63.5 us; the launch traced here: 63 us
  Pallas kernels  55.8 us (88%)
  local copies, waits for them, and re-layouts  4.51 us (7%)
  other arithmetic  1.81 us (3%)
  between operations  0.84 us (1%)
    pallas_call x1, Pallas kernels, spread_rows(): pl.pallas_call(functools.partial(spread_kernel, pass_count, cent_count, p...  24.7 us
    pallas_call x1, Pallas kernels, score_passages(): pl.pallas_call(functools.partial(score_kernel, passage_len), out_shape=ja...  16.6 us
    pallas_call x1, Pallas kernels, finish(): pl.pallas_call(functools.partial(finish_kernel, pass_count, cent_count),...  12.2 us
    pallas_call x1, Pallas kernels, largest(): pl.pallas_call(functools.partial(top_kernel, KTOP), out_shape=jax.ShapeDt...  2.31 us
    unnamed x13, local copies, waits for them, and re-layouts  1.62 us

profile of v5, /device:TPU:0, one launch (start us, length us, event | category | flops | bytes accessed | tf_op | source)
XLA Modules:
  0.0 63.0 jit_solution(4088511888065012309)
XLA Ops:
  0.6 0.0 copy-start
  0.7 0.7 %subtract_bitcast_fusion.wanted_ref = s32[1024]{0:T(1024)S(1)} fusion(s32[8,4096]{1,0:T(8,128)} %param.11, s32[]{:T(128)S(6)} %select_n.35, s32[]{:T(128)S(6)} %mul.15), kind=kLoop, calls=%fused_computation.17 | loop fusion | flops 1024 | bytes 8200 | tf_op jit(solution)/shard_map/reshape | solution.py:404
  1.4 0.9 %copy-done.1 = f32[8,32,128]{2,1,0:T(8,128)S(1)} copy-done((f32[8,32,128]{2,1,0:T(8,128)S(1)}, f32[8,32,128]{2,1,0:T(8,128)}, u32[]{:S(2)}) %copy-start.1) | copy-done | bytes 131096
  2.3 24.7 %shard_map.98 = (f32[32,128,128]{2,1,0:T(8,128)S(1)}, f32[4,8,32,128]{3,2,1,0:T(8,128)S(1)}) custom-call(s32[1024]{0:T(1024)S(1)} %subtract_bitcast_fusion.wanted_ref, f32[8192,128]{1,0:T(8,128)} %stored_ref.1, f32[8,32,128]{2,1,0:T(8,128)S(1)} %copy-done.1), custom_call_target="tpu_custom_call" | custom-call | tf_op jit(solution)/shard_map/pallas_call | solution.py:150
  27.0 0.2 copy.20
  27.2 0.1 reduce-precision_convert_fusion
  27.4 0.1 copy.26
  27.5 0.1 copy.19
  27.6 0.1 reshape.110.codes_ref
  27.8 16.6 %shard_map.99 = f32[32,128]{1,0:T(8,128)S(1)} custom-call(s32[1]{0:T(128)} %bitcast.2.where_ref, s32[8192]{0:T(1024)S(1)} %reshape.110.codes_ref, s32[512,2048]{1,0:T(8,128)} %bits_ref.1, f32[4,128]{1,0:T(4,128)S(1)} %copy-done.3, bf16[256,1024]{1,0:T(8,128)(2,1)S(1)} %maximum_bitcast_fusion.query_ref, f32[32,1024]{1,0:T(8,128)S(1)} %fusion.1.fold_ref, ...), custom_call_target="tpu_custom_call" | custom-call | tf_op jit(solution)/shard_map/pallas_call | solution.py:363
  44.4 0.6 copy-done.2
  45.0 0.1 iota_compare_fusion.2
  45.1 0.1 iota_compare_fusion.1
  45.2 0.1 broadcast_in_dim.46
  45.3 0.1 reshape_reshape.7
  45.5 0.6 copy.28
  46.1 12.2 %shard_map.100 = (f32[4,8,128]{2,1,0:T(8,128)}, f32[8,4,8,128]{3,2,1,0:T(8,128)}) custom-call(f32[4,8,128]{2,1,0:T(8,128)} %bitcast.19, s32[4,8,128]{2,1,0:T(8,128)} %bitcast.21), custom_call_target="tpu_custom_call" | custom-call | tf_op jit(solution)/shard_map/pallas_call | solution.py:274
  58.3 0.7 %copy.23 = f32[8,4,128]{2,1,0:T(4,128)S(1)} copy(f32[8,4,128]{2,0,1:T(8,128)} %bitcast.22) | data formatting | bytes 32768 | tf_op jit(solution)/shard_map/transpose | solution.py:425
  59.0 0.1 broadcast_in_dim.47
  59.1 0.1 copy.24
  59.2 0.6 select_reduce_fusion
  59.8 0.1 broadcast_select_fusion
  59.9 0.7 %select_n.40 = f32[8,1,512]{2,1,0:T(1,128)} reshape(f32[8,32,16]{2,1,0:T(8,128)S(1)} %broadcast_select_fusion) | data formatting | bytes 32768 | tf_op jit(solution)/shard_map/jit(_where)/select_n | solution.py:427
  60.7 2.3 %shard_map.101 = f32[8,32]{1,0:T(8,128)} custom-call(f32[8,4,8,128]{3,2,1,0:T(8,128)} %get-tuple-element.9.box_ref), custom_call_target="tpu_custom_call" | custom-call | tf_op jit(solution)/shard_map/pallas_call | solution.py:264
  (14 shorter events, 0.1 us)
Async XLA Ops:
  0.6 26.7 %copy-start = (s32[512,64]{0,1:T(8,128)S(1)}, s32[512,64]{0,1:T(8,128)}, u32[]{:S(2)}) copy-start(s32[512,64]{0,1:T(8,128)} %param.12) | copy-start | bytes 393220
  1.4 0.9 %copy-start.1 = (f32[8,32,128]{2,1,0:T(8,128)S(1)}, f32[8,32,128]{2,1,0:T(8,128)}, u32[]{:S(2)}) copy-start(f32[8,32,128]{2,1,0:T(8,128)} %queries_ref.1) | copy-start | bytes 393220
  27.0 0.8 %copy-start.3 = (f32[4,128]{1,0:T(4,128)S(1)}, f32[4,128]{1,0:T(4,128)}, u32[]{:S(2)}) copy-start(f32[4,128]{1,0:T(4,128)} %weights_ref.1) | copy-start | bytes 6148
  27.8 17.2 %copy-start.5 = (s32[8,1]{0,1:T(1,128)S(1)}, s32[8,1]{0,1:T(1,128)}, u32[]{:S(2)}) copy-start(s32[8,1]{0,1:T(1,128)} %param.15) | copy-start | bytes 100
  27.8 17.3 %copy-start.4 = (s32[8,1,32]{2,1,0:T(1,128)S(1)}, s32[8,1,32]{2,1,0:T(1,128)}, u32[]{:S(2)}) copy-start(s32[8,1,32]{2,1,0:T(1,128)} %param.14) | copy-start | bytes 3076
  44.4 0.6 copy-start.2
